TPU v7x, 512 devices: a whole 4x8x8 slice. The times are simulated.
512 devices in a mesh: dp: 64 (over x, y_lo, z), ctx: 8 (over y_hi, core).
Axes of the slice: x: 4, y: 8 (y_hi: 4, y_lo: 2; y = y_hi * 2 + y_lo), z: 8, core: 2. Of those that a mesh axis runs over, the one named last changes fastest.
Arguments:
- query_in: bfloat16 [64, 1024, 1024], P('dp', 'ctx'), may hold values from -6 to 6
- key_in: bfloat16 [64, 1024, 1024], P('dp', 'ctx'), may hold values from -6 to 6
- value_in: bfloat16 [64, 1024, 1024], P('dp', 'ctx'), may hold values from -6 to 6
- gate_in: bfloat16 [64, 1024, 1024], P('dp', 'ctx'), may hold values from -6 to 6
- out_grad: bfloat16 [64, 1024, 1024], P('dp', 'ctx'), may hold values from -6 to 6
- out_weight: bfloat16 [1024, 1024], P('dp'), may hold values from -0.1875 to 0.1875
- lengths: int32 [64, 8], P('dp'), may hold values from 1 to 512, 1024 in all within a row
- stamps: int32 [64, 1024], P('dp'), may hold values from 1 to 6291456, as said below
- pos_bias: float32 [1024], replicated, may hold values from -3 to 3
- time_bias: float32 [32], replicated, may hold values from -3 to 3
Outputs:
- layer_out: bfloat16 [64, 1024, 1024], P('dp', 'ctx')
- query_grad: bfloat16 [64, 1024, 1024], P('dp', 'ctx')
- key_grad: bfloat16 [64, 1024, 1024], P('dp', 'ctx')
- value_grad: bfloat16 [64, 1024, 1024], P('dp', 'ctx')
- gate_grad: bfloat16 [64, 1024, 1024], P('dp', 'ctx')
- weight_grad: float32 [1024, 1024], P('dp')
- pos_grad: float32 [1024], replicated
- time_grad: float32 [32], replicated
Inputs may be any that keep to these rules, and one draw needn't show every extreme that they name: In every pack the 8 lengths add up to 1024 and the longest is exactly 512. `stamps`: timestamps rise strictly along each pack; each pack's first is 1 and its last is 6291456.
All inputs are finite; a program needn't handle non-finite values.
Results may differ from a plain program's by a relative error of at most 0.015.
Values may be sent and summed in bfloat16 or wider, within the bound.
A program may use at most 64 MiB of HBM per device.

v0:
```python
import jax
import jax.numpy as jnp
from jax import lax
from jax.sharding import PartitionSpec as P

HEAD_DIM = 128
EPSILON = 1e-06


def bucket_of(time_gap):
    bucket = jnp.zeros(time_gap.shape, jnp.int32)
    for shift_by in range(31):
        bucket = bucket + (time_gap >= 1 << shift_by).astype(jnp.int32)
    return bucket


def toeplitz(table, offset, row_total, col_total):
    length = table.shape[0]
    extended = jnp.concatenate(
        [jnp.zeros((length + col_total,), table.dtype), table, jnp.zeros((row_total,), table.dtype)]
    )
    diag_span = row_total + col_total - 1
    window = lax.dynamic_slice_in_dim(extended, length + offset + 1, diag_span)
    flipped = window[::-1]
    repeated = jnp.tile(flipped, row_total + 1)[: row_total * (diag_span + 1)]
    sliding = repeated.reshape(row_total, diag_span + 1)[:, :col_total]
    return sliding[::-1]


def block_bias(pos_table, time_table, query_stamps, key_stamps, offset):
    row_total = query_stamps.shape[0]
    col_total = key_stamps.shape[0]
    bucket = bucket_of(jnp.abs(query_stamps[:, None] - key_stamps[None, :]))
    timed = jnp.zeros((row_total, col_total), jnp.float32)
    for bucket_no in range(time_table.shape[0]):
        timed = timed + jnp.where(bucket == bucket_no, time_table[bucket_no], 0.0)
    return toeplitz(pos_table, offset, row_total, col_total) + timed


def split_heads(block_rows):
    return block_rows.reshape(block_rows.shape[0], block_rows.shape[1] // HEAD_DIM, HEAD_DIM)


def score_grads(scores, pair_mask, grad_block, value_block):
    weight_grads = jnp.einsum(
        "rhd,chd->hrc",
        split_heads(grad_block),
        split_heads(value_block),
        preferred_element_type=jnp.float32,
    )
    gate_sig = jax.nn.sigmoid(scores)
    return jnp.where(
        pair_mask[None], weight_grads * gate_sig * (1.0 + scores * (1.0 - gate_sig)), 0.0
    )


def on_device(
    query_in, key_in, value_in, gate_in, out_grad, out_weight, lengths, stamps, pos_bias, time_bias
):
    query_mine = query_in[0]
    key_mine = key_in[0]
    value_mine = value_in[0]
    gate_mine = gate_in[0]
    grad_mine = out_grad[0]
    row_count = query_mine.shape[0]
    context = stamps.shape[1]
    stamp_row = stamps[0]
    user_ends = jnp.cumsum(lengths[0])
    places = lax.iota(jnp.int32, context)
    user_ids = jnp.sum((places[:, None] >= user_ends[None, :]).astype(jnp.int32), axis=1)
    my_first = lax.axis_index("ctx") * row_count
    factor = HEAD_DIM ** (-0.5)

    def pair_terms(query_block, key_block, query_first, key_first):
        query_size = query_block.shape[0]
        key_size = key_block.shape[0]
        query_users = lax.dynamic_slice_in_dim(user_ids, query_first, query_size)
        key_users = lax.dynamic_slice_in_dim(user_ids, key_first, key_size)
        query_stamps = lax.dynamic_slice_in_dim(stamp_row, query_first, query_size)
        key_stamps = lax.dynamic_slice_in_dim(stamp_row, key_first, key_size)
        query_places = query_first + lax.iota(jnp.int32, query_size)
        key_places = key_first + lax.iota(jnp.int32, key_size)
        pair_mask = (query_users[:, None] == key_users[None, :]) & (
            query_places[:, None] >= key_places[None, :]
        )

        def bias_of(table_pos, table_time):
            return block_bias(
                table_pos, table_time, query_stamps, key_stamps, query_first - key_first
            )

        pair_bias, pull_back = jax.vjp(bias_of, pos_bias, time_bias)
        scores = (
            jnp.einsum(
                "rhd,chd->hrc",
                split_heads(query_block),
                split_heads(key_block),
                preferred_element_type=jnp.float32,
            )
            * factor
            + pair_bias[None]
        )
        return (scores, pair_mask, pull_back)

    key_all, value_all = (
        lax.all_gather(key_mine, "ctx", axis=0, tiled=True),
        lax.all_gather(value_mine, "ctx", axis=0, tiled=True),
    )
    query_size = min(512, query_mine.shape[0])
    key_size = min(512, key_all.shape[0])
    col_count = query_mine.shape[1]

    def forward_per_query(query_step):
        query_start = my_first + query_step * query_size

        def forward_per_key(carried, key_step):
            key_start = 0 + key_step * key_size
            key_block = lax.dynamic_slice_in_dim(key_all, key_step * key_size, key_size)
            value_block = lax.dynamic_slice_in_dim(value_all, key_step * key_size, key_size)
            scores, pair_mask, pull_back = pair_terms(query_mine, key_block, query_start, key_start)
            weights = jnp.where(pair_mask[None], jax.nn.silu(scores), 0.0).astype(jnp.bfloat16)
            attended_part = jnp.einsum(
                "hrc,chd->rhd",
                weights,
                split_heads(value_block),
                preferred_element_type=jnp.float32,
            )
            return (carried + attended_part.reshape(query_size, col_count), None)

        zeros_init = jnp.zeros((query_size, col_count), jnp.float32)
        result, unused = lax.scan(
            forward_per_key, zeros_init, lax.iota(jnp.int32, key_all.shape[0] // key_size)
        )
        return result

    outputs = lax.map(forward_per_query, lax.iota(jnp.int32, query_mine.shape[0] // query_size))
    attended = outputs.reshape(query_mine.shape).astype(jnp.bfloat16)
    attended_wide = attended.astype(jnp.float32)
    center = attended_wide - jnp.mean(attended_wide, axis=1, keepdims=True)
    inv_dev = lax.rsqrt(jnp.mean(center * center, axis=1, keepdims=True) + EPSILON)
    normed = center * inv_dev
    gate_wide = gate_mine.astype(jnp.float32)
    mixed_rows = (normed * gate_wide).astype(jnp.bfloat16)
    contract_cols = (((1,), (1,)), ((), ()))
    whole_rows = lax.all_gather(out_weight, "dp", axis=0, tiled=True)
    layer_out = jnp.dot(mixed_rows, whole_rows, preferred_element_type=jnp.float32)
    mixed_grad = lax.dot_general(
        grad_mine, whole_rows, contract_cols, preferred_element_type=jnp.float32
    )
    weight_part = lax.psum_scatter(
        lax.dot_general(
            mixed_rows, grad_mine, (((0,), (0,)), ((), ())), preferred_element_type=jnp.float32
        ),
        "dp",
        scatter_dimension=0,
        tiled=True,
    )
    weight_grad = lax.psum(weight_part, "ctx")
    gate_grad = (mixed_grad * normed).astype(jnp.bfloat16)
    normed_grad = mixed_grad * gate_wide
    attn_grad = inv_dev * (
        normed_grad
        - jnp.mean(normed_grad, axis=1, keepdims=True)
        - normed * jnp.mean(normed_grad * normed, axis=1, keepdims=True)
    )
    attn_grad = attn_grad.astype(jnp.bfloat16)
    grad_rows = attn_grad
    query_query_size = min(512, query_mine.shape[0])
    query_key_size = min(512, key_all.shape[0])
    query_col_count = query_mine.shape[1]

    def query_per_query(query_step):
        query_start = my_first + query_step * query_query_size

        def query_per_key(carried, key_step):
            key_start = 0 + key_step * query_key_size
            key_block = lax.dynamic_slice_in_dim(key_all, key_step * query_key_size, query_key_size)
            value_block = lax.dynamic_slice_in_dim(
                value_all, key_step * query_key_size, query_key_size
            )
            scores, pair_mask, pull_back = pair_terms(query_mine, key_block, query_start, key_start)
            score_grad = score_grads(scores, pair_mask, grad_rows, value_block)
            pos_part, time_part = pull_back(jnp.sum(score_grad, axis=0))
            query_part = jnp.einsum(
                "hrc,chd->rhd",
                score_grad.astype(jnp.bfloat16),
                split_heads(key_block),
                preferred_element_type=jnp.float32,
            )
            return (
                (
                    carried[0] + query_part.reshape(query_query_size, query_col_count),
                    carried[1] + pos_part,
                    carried[2] + time_part,
                ),
                None,
            )

        zeros_init = (
            jnp.zeros((query_query_size, query_col_count), jnp.float32),
            jnp.zeros(pos_bias.shape, jnp.float32),
            jnp.zeros(time_bias.shape, jnp.float32),
        )
        result, unused = lax.scan(
            query_per_key, zeros_init, lax.iota(jnp.int32, key_all.shape[0] // query_key_size)
        )
        return result

    query_sums, pos_sums, time_sums = lax.map(
        query_per_query, lax.iota(jnp.int32, query_mine.shape[0] // query_query_size)
    )
    query_grad = (query_sums.reshape(query_mine.shape) * factor).astype(jnp.bfloat16)
    query_grad, pos_local, time_local = (
        query_grad,
        jnp.sum(pos_sums, axis=0),
        jnp.sum(time_sums, axis=0),
    )
    query_all, grad_all = (
        lax.all_gather(query_mine, "ctx", axis=0, tiled=True),
        lax.all_gather(attn_grad, "ctx", axis=0, tiled=True),
    )
    key_query_size = min(512, query_all.shape[0])
    key_key_size = min(512, key_mine.shape[0])
    key_col_count = key_mine.shape[1]

    def key_per_key(key_step):
        key_start = my_first + key_step * key_key_size

        def per_per_query(carried, query_step):
            query_start = 0 + query_step * key_query_size
            query_block = lax.dynamic_slice_in_dim(
                query_all, query_step * key_query_size, key_query_size
            )
            grad_block = lax.dynamic_slice_in_dim(
                grad_all, query_step * key_query_size, key_query_size
            )
            scores, pair_mask, pull_back = pair_terms(query_block, key_mine, query_start, key_start)
            weights = jnp.where(pair_mask[None], jax.nn.silu(scores), 0.0).astype(jnp.bfloat16)
            score_grad = score_grads(scores, pair_mask, grad_block, value_mine)
            value_part = jnp.einsum(
                "hrc,rhd->chd", weights, split_heads(grad_block), preferred_element_type=jnp.float32
            )
            key_part = jnp.einsum(
                "hrc,rhd->chd",
                score_grad.astype(jnp.bfloat16),
                split_heads(query_block),
                preferred_element_type=jnp.float32,
            )
            return (
                (
                    carried[0] + key_part.reshape(key_key_size, key_col_count),
                    carried[1] + value_part.reshape(key_key_size, key_col_count),
                ),
                None,
            )

        zero_rows = jnp.zeros((key_key_size, key_col_count), jnp.float32)
        result, unused = lax.scan(
            per_per_query,
            (zero_rows, zero_rows),
            lax.iota(jnp.int32, query_all.shape[0] // key_query_size),
        )
        return result

    key_sums, value_sums = lax.map(
        key_per_key, lax.iota(jnp.int32, key_mine.shape[0] // key_key_size)
    )
    key_grad = (key_sums.reshape(key_mine.shape) * factor).astype(jnp.bfloat16)
    key_grad, value_grad = (key_grad, value_sums.reshape(key_mine.shape).astype(jnp.bfloat16))
    pos_grad, time_grad = lax.psum((pos_local, time_local), ("dp", "ctx"))
    return (
        layer_out.astype(jnp.bfloat16)[None],
        query_grad[None],
        key_grad[None],
        value_grad[None],
        gate_grad[None],
        weight_grad,
        pos_grad,
        time_grad,
    )


def solution(mesh):
    placed = (
        P("dp", "ctx", None),
        P("dp", "ctx", None),
        P("dp", "ctx", None),
        P("dp", "ctx", None),
        P("dp", "ctx", None),
        P("dp", None),
        P("dp", None),
        P("dp", None),
        P(),
        P(),
    )
    return jax.shard_map(
        on_device,
        mesh=mesh,
        in_specs=placed,
        out_specs=(
            P("dp", "ctx", None),
            P("dp", "ctx", None),
            P("dp", "ctx", None),
            P("dp", "ctx", None),
            P("dp", "ctx", None),
            P("dp", None),
            P(),
            P(),
        ),
        check_vma=False,
    )
```

profile of v0, /device:TPU:17, one launch (start us, length us, event | category | flops | bytes accessed | tf_op | source)
XLA Modules:
  0.0 894.1 jit_solution(12226835931457690420)
XLA Ops:
  14.1 43.6 %all-gather.13.cloned.1.call-done = bf16[1,1024,1024]{1,2,0:T(8,128)(2,1)} async-done(((bf16[1,128,1024]{1,2,0:T(8,128)(2,1)}), bf16[1,1024,1024]{1,2,0:T(8,128)(2,1)}) %all-gather.13.cloned.1.call-update) | async-done | bytes 2097168 | tf_op jit(solution)/shard_map/all_gather | solution.py:107
  57.7 44.1 %all-gather.15.cloned.1.call-done = bf16[1,1024,1024]{1,2,0:T(8,128)(2,1)} async-done(((bf16[1,128,1024]{1,2,0:T(8,128)(2,1)}), bf16[1,1024,1024]{1,2,0:T(8,128)(2,1)}) %all-gather.15.cloned.1.call-update) | async-done | bytes 2097168 | tf_op jit(solution)/shard_map/all_gather | solution.py:106
  101.8 72.8 %while.78 = (s32[]{:T(128)}, f32[128,1024]{0,1:T(8,128)}, s32[2]{0:T(128)S(1)}, bf16[1024,1024]{0,1:T(8,128)(2,1)}, s32[128]{0:T(128)S(1)}, /*index=5*/s32[1024]...) while((s32[]{:T(128)}, f32[128,1024]{0,1:T(8,128)}, ...), condition=%wide.region_3.4_spmd.clone, body=%wide.region_2.3_spmd.clone.sunk | while | flops 285542272 | bytes 18211576 | solution.py:131
  109.5 21.8 %add_add_fusion.6 = f32[128,512]{1,0:T(8,128)S(1)} fusion(f32[128,512]{1,0:T(8,128)S(1)} %rev.84, f32[]{:T(128)} %bitcast.417, f32[]{:T(128)} %bitcast.418, f32[]{:T(128)} %bitcast.419, f32[]{:T(128)} %bitcast.420, f32[]{:T(128)} %bitcast.421, f32[]{:T(128)} %bitcast.422, f32[]{:T(128)} %bitcast.423, f32[]{:T(128)} %bitcast.424, f32[]{:T(128)} %bitcast.425, ...), kind=kLoop, calls=%fused_computation.10.clone.1 | loop fusion | flops 12451840 | bytes 526976 | tf_op jit(solution)/shard_map/while/body/eval_jaxpr/while/body/eval_jaxpr/jvp()/add | solution.py:37
  133.2 3.1 fusion.217
  145.9 21.8 %add_add_fusion.6 = f32[128,512]{1,0:T(8,128)S(1)} fusion(f32[128,512]{1,0:T(8,128)S(1)} %rev.84, f32[]{:T(128)} %bitcast.417, f32[]{:T(128)} %bitcast.418, f32[]{:T(128)} %bitcast.419, f32[]{:T(128)} %bitcast.420, f32[]{:T(128)} %bitcast.421, f32[]{:T(128)} %bitcast.422, f32[]{:T(128)} %bitcast.423, f32[]{:T(128)} %bitcast.424, f32[]{:T(128)} %bitcast.425, ...), kind=kLoop, calls=%fused_computation.10.clone.1 | loop fusion | flops 12451840 | bytes 526976 | tf_op jit(solution)/shard_map/while/body/eval_jaxpr/while/body/eval_jaxpr/jvp()/add | solution.py:37
  169.6 3.1 fusion.217
  176.2 185.8 %all-gather.9.cloned.1.call-done = bf16[1024,1024]{1,0:T(8,128)(2,1)} async-done(((bf16[16,1024]{1,0:T(8,128)(2,1)}), bf16[1024,1024]{1,0:T(8,128)(2,1)}) %all-gather.9.cloned.1.call-update) | async-done | bytes 2097168 | tf_op jit(solution)/shard_map/all_gather | solution.py:145
  362.0 2.5 fusion.156
  365.8 2.8 fusion.152
  370.1 150.5 %while.79 = (s32[]{:T(128)}, f32[128,1024]{0,1:T(8,128)}, f32[1024]{0:T(1024)S(1)}, f32[32]{0:T(128)S(1)}, s32[2]{0:T(128)S(1)}, /*index=5*/bf16[1024,1024]{0,1:...) while((s32[]{:T(128)}, f32[128,1024]{0,1:T(8,128)}, ...), condition=%wide.region_43.44_spmd.clone, body=%wide.region_8.43_spmd.clone.sunk | while | flops 434852608 | bytes 32417576 | solution.py:204
  383.9 3.1 rev.85
  388.5 22.5 %add_add_fusion.7 = f32[128,512]{0,1:T(8,128)S(1)} fusion(f32[128,512]{0,1:T(8,128)} %rev.85, f32[]{:T(128)} %bitcast.461, f32[]{:T(128)} %bitcast.462, f32[]{:T(128)} %bitcast.463, f32[]{:T(128)} %bitcast.464, f32[]{:T(128)} %bitcast.465, f32[]{:T(128)} %bitcast.466, f32[]{:T(128)} %bitcast.467, f32[]{:T(128)} %bitcast.468, f32[]{:T(128)} %bitcast.469, ...), kind=kLoop, calls=%fused_computation.100.clone.1 | loop fusion | flops 12451840 | bytes 526976 | tf_op jit(solution)/shard_map/while/body/eval_jaxpr/while/body/eval_jaxpr/jvp()/add | solution.py:37
  422.7 2.5 select_reduce_fusion.33
  425.2 20.1 %fusion.230 = f32[32]{0:T(128)S(1)} fusion(f32[32]{0:T(128)S(1)} %get-tuple-element.2032, pred[]{:T(512)S(6)} %compare.44, f32[1]{0:T(128)} %bitcast.497, f32[1]{0:T(128)} %bitcast.498, f32[1]{0:T(128)} %bitcast.499, f32[1]{0:T(128)} %bitcast.500, f32[1]{0:T(128)} %bitcast.501, f32[1]{0:T(128)} %bitcast.502, f32[1]{0:T(128)} %bitcast.503, ...), kind=kLoop, calls=%fused_computation.175.clone.1 | loop fusion | flops 1056 | bytes 385 | tf_op jit(solution)/shard_map/while/body/eval_jaxpr/while/body/eval_jaxpr/add | solution.py:194
  446.6 2.5 constant_dynamic-slice_fusion.11
  459.1 3.1 rev.85
  463.7 22.5 %add_add_fusion.7 = f32[128,512]{0,1:T(8,128)S(1)} fusion(f32[128,512]{0,1:T(8,128)} %rev.85, f32[]{:T(128)} %bitcast.461, f32[]{:T(128)} %bitcast.462, f32[]{:T(128)} %bitcast.463, f32[]{:T(128)} %bitcast.464, f32[]{:T(128)} %bitcast.465, f32[]{:T(128)} %bitcast.466, f32[]{:T(128)} %bitcast.467, f32[]{:T(128)} %bitcast.468, f32[]{:T(128)} %bitcast.469, ...), kind=kLoop, calls=%fused_computation.100.clone.1 | loop fusion | flops 12451840 | bytes 526976 | tf_op jit(solution)/shard_map/while/body/eval_jaxpr/while/body/eval_jaxpr/jvp()/add | solution.py:37
  498.1 2.5 select_reduce_fusion.33
  500.6 20.1 %fusion.230 = f32[32]{0:T(128)S(1)} fusion(f32[32]{0:T(128)S(1)} %get-tuple-element.2032, pred[]{:T(512)S(6)} %compare.44, f32[1]{0:T(128)} %bitcast.497, f32[1]{0:T(128)} %bitcast.498, f32[1]{0:T(128)} %bitcast.499, f32[1]{0:T(128)} %bitcast.500, f32[1]{0:T(128)} %bitcast.501, f32[1]{0:T(128)} %bitcast.502, f32[1]{0:T(128)} %bitcast.503, ...), kind=kLoop, calls=%fused_computation.175.clone.1 | loop fusion | flops 1056 | bytes 385 | tf_op jit(solution)/shard_map/while/body/eval_jaxpr/while/body/eval_jaxpr/add | solution.py:194
  521.9 141.3 %all-reduce.34 = (f32[1024]{0:T(1024)}, f32[32]{0:T(128)}) all-reduce(f32[1024]{0:T(1024)S(1)} %get-tuple-element.956, f32[32]{0:T(128)S(1)} %get-tuple-element.957), channel_id=1, replica_groups=mesh['dp'=64,'ctx'=8] {'dp','ctx'}, use_global_device_ids=true, to_apply=%region_48.49 | all-reduce | flops 1056 | bytes 8448 | tf_op jit(solution)/shard_map/psum | solution.py:270
  663.2 3.0 fusion.136
  666.9 88.4 %while.80 = (s32[]{:T(128)}, f32[128,1024]{0,1:T(8,128)}, f32[128,1024]{0,1:T(8,128)}, s32[2]{0:T(128)S(1)}, bf16[1024,1024]{0,1:T(8,128)(2,1)}, /*index=5*/s32[...) while((s32[]{:T(128)}, f32[128,1024]{0,1:T(8,128)}, ...), condition=%wide.region_45.46_spmd.clone, body=%wide.region_44.45_spmd.clone.sunk | while | flops 560531328 | bytes 61329784 | solution.py:258
  677.5 21.7 %add_add_fusion.8 = f32[512,128]{1,0:T(8,128)S(1)} fusion(f32[512,128]{1,0:T(8,128)S(1)} %rev.87, f32[]{:T(128)} %bitcast.540, f32[]{:T(128)} %bitcast.541, f32[]{:T(128)} %bitcast.542, f32[]{:T(128)} %bitcast.543, f32[]{:T(128)} %bitcast.544, f32[]{:T(128)} %bitcast.545, f32[]{:T(128)} %bitcast.546, f32[]{:T(128)} %bitcast.547, f32[]{:T(128)} %bitcast.548, ...), kind=kLoop, calls=%fused_computation.195.clone.1 | loop fusion | flops 12451840 | bytes 526976 | tf_op jit(solution)/shard_map/while/body/eval_jaxpr/while/body/eval_jaxpr/jvp()/add | solution.py:37
  699.5 3.8 fusion.241
  705.1 3.6 fusion.242
  721.5 21.7 %add_add_fusion.8 = f32[512,128]{1,0:T(8,128)S(1)} fusion(f32[512,128]{1,0:T(8,128)S(1)} %rev.87, f32[]{:T(128)} %bitcast.540, f32[]{:T(128)} %bitcast.541, f32[]{:T(128)} %bitcast.542, f32[]{:T(128)} %bitcast.543, f32[]{:T(128)} %bitcast.544, f32[]{:T(128)} %bitcast.545, f32[]{:T(128)} %bitcast.546, f32[]{:T(128)} %bitcast.547, f32[]{:T(128)} %bitcast.548, ...), kind=kLoop, calls=%fused_computation.195.clone.1 | loop fusion | flops 12451840 | bytes 526976 | tf_op jit(solution)/shard_map/while/body/eval_jaxpr/while/body/eval_jaxpr/jvp()/add | solution.py:37
  743.6 3.8 fusion.241
  749.1 3.6 fusion.242
  752.7 2.6 bitcast_add_fusion.11
  756.6 7.0 reduce-scatter.2.cloned.1.call-done
  765.2 120.6 %all-reduce.37.cloned.1.call-done = f32[16,1024]{1,0:T(8,128)} async-done(((f32[16,1024]{1,0:T(8,128)}), f32[16,1024]{1,0:T(8,128)}) %all-reduce.37.cloned.1.call-update) | async-done | bytes 65552 | tf_op jit(solution)/shard_map/psum | solution.py:158
  (277 shorter events, 114.9 us)
Async XLA Ops:
  7.2 354.9 %copy-start = (bf16[1,128,1024]{2,1,0:T(8,128)(2,1)S(1)}, bf16[1,128,1024]{2,1,0:T(8,128)(2,1)}, u32[]{:S(2)}) copy-start(bf16[1,128,1024]{2,1,0:T(8,128)(2,1)} %param.20) | copy-start | bytes 786436
  7.2 94.6 %copy-start.6 = (bf16[1,128,1024]{2,1,0:T(8,128)(2,1)S(1)}, bf16[1,128,1024]{2,1,0:T(8,128)(2,1)}, u32[]{:S(2)}) copy-start(bf16[1,128,1024]{2,1,0:T(8,128)(2,1)} %param.16) | copy-start | bytes 786436
  7.2 6.5 copy-start.20
  7.2 6.9 copy-start.19
  7.2 94.6 %copy-start.18 = (f32[1024]{0:T(1024)S(1)}, f32[1024]{0:T(1024)}, u32[]{:S(2)}) copy-start(f32[1024]{0:T(1024)} %param.24) | copy-start | bytes 12292
  7.2 94.6 %copy-start.1 = (f32[32]{0:T(128)S(1)}, f32[32]{0:T(128)}, u32[]{:S(2)}) copy-start(f32[32]{0:T(128)} %param.25) | copy-start | bytes 388
  7.2 50.4 %all-gather.13.cloned.1.call-start = ((), (), s32[]{:S(2)}) async-start(), calls=%async_computation.5 | async-start | bytes 2359296 | tf_op jit(solution)/shard_map/all_gather | solution.py:107
  9.2 92.6 %all-gather.15.cloned.1.call-start = ((), (), s32[]{:S(2)}) async-start(), calls=%async_computation.6 | async-start | bytes 2359296 | tf_op jit(solution)/shard_map/all_gather | solution.py:106
  11.1 351.0 %all-gather.9.cloned.1.call-start = ((), (), s32[]{:S(2)}) async-start(), calls=%async_computation.1 | async-start | bytes 2129920 | tf_op jit(solution)/shard_map/all_gather | solution.py:145
  11.8 655.2 %all-gather.17.cloned.1.call-start = ((), (), s32[]{:S(2)}) async-start(), calls=%async_computation.7 | async-start | bytes 2359296 | tf_op jit(solution)/shard_map/all_gather | solution.py:219
  13.7 653.3 %all-gather.11.cloned.1.call-start = ((), (), s32[]{:S(2)}) async-start(), calls=%async_computation.2 | async-start | bytes 2359296 | tf_op jit(solution)/shard_map/all_gather | solution.py:220
  133.2 3.1 copy-start.9
  169.6 3.1 copy-start.9
  175.9 189.9 %copy-start.13 = (bf16[128,1024]{1,0:T(8,128)(2,1)}, bf16[128,1024]{1,0:T(8,128)(2,1)S(1)}, u32[]{:S(2)}) copy-start(bf16[128,1024]{1,0:T(8,128)(2,1)S(1)} %copy.114) | copy-start | bytes 786436
  175.9 188.7 %copy-start.16 = (bf16[1,128,1024]{2,1,0:T(8,128)(2,1)S(1)}, bf16[1,128,1024]{2,1,0:T(8,128)(2,1)}, u32[]{:S(2)}) copy-start(bf16[1,128,1024]{2,1,0:T(8,128)(2,1)} %param.19) | copy-start | bytes 786436
  365.7 397.9 %reduce-scatter.2.cloned.1.call-start = ((), (), s32[]{:S(2)}) async-start(), calls=%async_computation.3 | async-start | bytes 4259840 | tf_op jit(solution)/shard_map/reduce_scatter | solution.py:150
  368.6 517.2 %all-reduce.37.cloned.1.call-start = ((), (), s32[]{:S(2)}) async-start(), calls=%async_computation.4 | async-start | bytes 131072 | tf_op jit(solution)/shard_map/psum | solution.py:158
  410.9 2.0 copy-start.17
  418.1 4.6 copy-start.8
  486.2 2.0 copy-start.17
  493.5 4.6 copy-start.8
  668.2 2.8 copy-start.12
  671.1 3.0 copy-start.2
  699.2 4.1 copy-start.15
  699.5 5.5 copy-start.3
  699.5 5.5 copy-start.5
  712.2 2.8 copy-start.12
  715.1 3.0 copy-start.2
  743.2 4.1 copy-start.15
  743.6 5.5 copy-start.3
  743.6 5.5 copy-start.5
  755.3 9.1 %copy-start.11 = (f32[128,1024]{0,1:T(8,128)S(1)}, f32[128,1024]{0,1:T(8,128)}, u32[]{:S(2)}) copy-start(f32[128,1024]{0,1:T(8,128)} %get-tuple-element.955) | copy-start | bytes 1572868
  (7 other events, 9.0 us)
Sparse Core Ops, SparseCore 0:
  10.8 46.8 all-gather.12
  60.4 41.4 all-gather.14
  103.9 258.0 all-gather.8
  364.0 82.6 all-gather.16
  449.3 37.8 all-gather.10
  489.8 273.7 reduce-scatter.1
  766.8 119.0 all-reduce.36
where the time goes:
time: 899 us; the launch traced here: 894 us
  waiting for transfers between devices  402 us (45%)
  other arithmetic  193 us (21%)
  blocking collectives  141 us (16%)
  local copies, waits for them, and re-layouts  97.3 us (11%)
  matrix products  40.8 us (5%)
  between operations  14.3 us (2%)
    all_gather x1, waiting for transfers between devices, on_device(): whole_rows = lax.all_gather(out_weight, 'dp', axis=0, tiled=True)  186 us
    psum x1, blocking collectives, on_device(): pos_grad, time_grad = lax.psum((pos_local, time_local), ('dp', 'ctx'))  141 us
    add x6, other arithmetic, block_bias(): return toeplitz(pos_table, offset, row_total, col_total) + timed  132 us
    psum x1, waiting for transfers between devices, on_device(): weight_grad = lax.psum(weight_part, 'ctx')  121 us
    all_gather x1, waiting for transfers between devices, on_device(): lax.all_gather(key_mine, 'ctx', axis=0, tiled=True)  44.1 us
    all_gather x1, waiting for transfers between devices, on_device(): lax.all_gather(value_mine, 'ctx', axis=0, tiled=True)  43.6 us
    add x2, other arithmetic, query_per_key(): carried[2] + time_part  40.2 us
  transfers between devices with their start and end apart: 7, of which 5 were waited for; matrix products, arithmetic and copies ran while one was open for 36% of the time, Pallas kernels for 0%

commit v1 on v0

--- a/solution.py
+++ b/solution.py
@@ -1,3 +1,4 @@
+import functools
 import jax
 import jax.numpy as jnp
 from jax import lax
@@ -5,6 +6,13 @@
 
 HEAD_DIM = 128
 EPSILON = 1e-06
+
+
+def plate_detail(slab_in, across):
+    return jnp.sum(jax.lax.all_gather(slab_in, across), axis=0)
+
+
+raise_the_loops = functools.partial(plate_detail, across="ctx")
 
 
 def bucket_of(time_gap):
@@ -155,7 +163,7 @@
         scatter_dimension=0,
         tiled=True,
     )
-    weight_grad = lax.psum(weight_part, "ctx")
+    weight_grad = raise_the_loops(weight_part)
     gate_grad = (mixed_grad * normed).astype(jnp.bfloat16)
     normed_grad = mixed_grad * gate_wide
     attn_grad = inv_dev * (

time: 899 us -> 843 us (0.938)
  the two profiles are of different devices: /device:TPU:17 before, /device:TPU:1 now
where the time goes in v1:
time: 843 us; the launch traced here: 839 us
  waiting for transfers between devices  285 us (34%)
  blocking collectives  207 us (25%)
  other arithmetic  194 us (23%)
  local copies, waits for them, and re-layouts  92.8 us (11%)
  matrix products  40.7 us (5%)
  between operations  14.3 us (2%)
    all_gather x1, waiting for transfers between devices, on_device(): whole_rows = lax.all_gather(out_weight, 'dp', axis=0, tiled=True)  189 us
    psum x1, blocking collectives, on_device(): pos_grad, time_grad = lax.psum((pos_local, time_local), ('dp', 'ctx'))  142 us
    add x6, other arithmetic, block_bias(): return toeplitz(pos_table, offset, row_total, col_total) + timed  132 us
    all_gather x1, blocking collectives, plate_detail(): return jnp.sum(jax.lax.all_gather(slab_in, across), axis=0)  65.4 us
    all_gather x1, waiting for transfers between devices, on_device(): lax.all_gather(value_mine, 'ctx', axis=0, tiled=True)  45.8 us
    all_gather x1, waiting for transfers between devices, on_device(): lax.all_gather(key_mine, 'ctx', axis=0, tiled=True)  44.1 us
    add x2, other arithmetic, query_per_key(): carried[2] + time_part  40.2 us
    while x70, local copies, waits for them, and re-layouts  18.9 us
  transfers between devices with their start and end apart: 6, of which 4 were waited for; matrix products, arithmetic and copies ran while one was open for 38% of the time, Pallas kernels for 0%

profile of v1, /device:TPU:1, one launch (start us, length us, event | category | flops | bytes accessed | tf_op | source)
XLA Modules:
  0.0 838.9 jit_solution(15680357455193889982)
XLA Ops:
  14.0 45.8 %all-gather.14.cloned.1.call-done = bf16[1,1024,1024]{1,2,0:T(8,128)(2,1)} async-done(((bf16[1,128,1024]{1,2,0:T(8,128)(2,1)}), bf16[1,1024,1024]{1,2,0:T(8,128)(2,1)}) %all-gather.14.cloned.1.call-update) | async-done | bytes 2097168 | tf_op jit(solution)/shard_map/all_gather | solution.py:115
  59.8 44.1 %all-gather.16.cloned.1.call-done = bf16[1,1024,1024]{1,2,0:T(8,128)(2,1)} async-done(((bf16[1,128,1024]{1,2,0:T(8,128)(2,1)}), bf16[1,1024,1024]{1,2,0:T(8,128)(2,1)}) %all-gather.16.cloned.1.call-update) | async-done | bytes 2097168 | tf_op jit(solution)/shard_map/all_gather | solution.py:114
  104.0 68.7 %while.78 = (s32[]{:T(128)}, f32[128,1024]{0,1:T(8,128)}, s32[2]{0:T(128)S(1)}, bf16[1024,1024]{0,1:T(8,128)(2,1)}, s32[128]{0:T(128)S(1)}, /*index=5*/s32[1024]...) while((s32[]{:T(128)}, f32[128,1024]{0,1:T(8,128)}, ...), condition=%wide.region_3.4_spmd.clone, body=%wide.region_2.3_spmd.clone.sunk | while | flops 285542272 | bytes 18211576 | solution.py:139
  109.4 21.8 %add_add_fusion.6 = f32[128,512]{1,0:T(8,128)S(1)} fusion(f32[128,512]{1,0:T(8,128)S(1)} %rev.84, f32[]{:T(128)} %bitcast.418, f32[]{:T(128)} %bitcast.419, f32[]{:T(128)} %bitcast.420, f32[]{:T(128)} %bitcast.421, f32[]{:T(128)} %bitcast.422, f32[]{:T(128)} %bitcast.423, f32[]{:T(128)} %bitcast.424, f32[]{:T(128)} %bitcast.425, f32[]{:T(128)} %bitcast.426, ...), kind=kLoop, calls=%fused_computation.10.clone.1 | loop fusion | flops 12451840 | bytes 526976 | tf_op jit(solution)/shard_map/while/body/eval_jaxpr/while/body/eval_jaxpr/jvp()/add | solution.py:45
  133.3 3.0 fusion.217
  143.7 21.8 %add_add_fusion.6 = f32[128,512]{1,0:T(8,128)S(1)} fusion(f32[128,512]{1,0:T(8,128)S(1)} %rev.84, f32[]{:T(128)} %bitcast.418, f32[]{:T(128)} %bitcast.419, f32[]{:T(128)} %bitcast.420, f32[]{:T(128)} %bitcast.421, f32[]{:T(128)} %bitcast.422, f32[]{:T(128)} %bitcast.423, f32[]{:T(128)} %bitcast.424, f32[]{:T(128)} %bitcast.425, f32[]{:T(128)} %bitcast.426, ...), kind=kLoop, calls=%fused_computation.10.clone.1 | loop fusion | flops 12451840 | bytes 526976 | tf_op jit(solution)/shard_map/while/body/eval_jaxpr/while/body/eval_jaxpr/jvp()/add | solution.py:45
  167.6 3.0 fusion.217
  174.2 188.8 %all-gather.10.cloned.1.call-done = bf16[1024,1024]{1,0:T(8,128)(2,1)} async-done(((bf16[16,1024]{1,0:T(8,128)(2,1)}), bf16[1024,1024]{1,0:T(8,128)(2,1)}) %all-gather.10.cloned.1.call-update) | async-done | bytes 2097168 | tf_op jit(solution)/shard_map/all_gather | solution.py:153
  363.0 2.5 fusion.156
  367.0 2.8 fusion.152
  371.3 150.5 %while.79 = (s32[]{:T(128)}, f32[128,1024]{0,1:T(8,128)}, f32[1024]{0:T(1024)S(1)}, f32[32]{0:T(128)S(1)}, s32[2]{0:T(128)S(1)}, /*index=5*/bf16[1024,1024]{0,1:...) while((s32[]{:T(128)}, f32[128,1024]{0,1:T(8,128)}, ...), condition=%wide.region_43.44_spmd.clone, body=%wide.region_8.43_spmd.clone.sunk | while | flops 434852608 | bytes 32417576 | solution.py:212
  385.0 3.1 rev.85
  389.6 22.5 %add_add_fusion.7 = f32[128,512]{0,1:T(8,128)S(1)} fusion(f32[128,512]{0,1:T(8,128)} %rev.85, f32[]{:T(128)} %bitcast.462, f32[]{:T(128)} %bitcast.463, f32[]{:T(128)} %bitcast.464, f32[]{:T(128)} %bitcast.465, f32[]{:T(128)} %bitcast.466, f32[]{:T(128)} %bitcast.467, f32[]{:T(128)} %bitcast.468, f32[]{:T(128)} %bitcast.469, f32[]{:T(128)} %bitcast.470, ...), kind=kLoop, calls=%fused_computation.100.clone.1 | loop fusion | flops 12451840 | bytes 526976 | tf_op jit(solution)/shard_map/while/body/eval_jaxpr/while/body/eval_jaxpr/jvp()/add | solution.py:45
  423.9 2.5 select_reduce_fusion.33
  426.4 20.1 %fusion.230 = f32[32]{0:T(128)S(1)} fusion(f32[32]{0:T(128)S(1)} %get-tuple-element.2032, pred[]{:T(512)S(6)} %compare.44, f32[1]{0:T(128)} %bitcast.498, f32[1]{0:T(128)} %bitcast.499, f32[1]{0:T(128)} %bitcast.500, f32[1]{0:T(128)} %bitcast.501, f32[1]{0:T(128)} %bitcast.502, f32[1]{0:T(128)} %bitcast.503, f32[1]{0:T(128)} %bitcast.504, ...), kind=kLoop, calls=%fused_computation.175.clone.1 | loop fusion | flops 1056 | bytes 385 | tf_op jit(solution)/shard_map/while/body/eval_jaxpr/while/body/eval_jaxpr/add | solution.py:202
  447.7 2.5 constant_dynamic-slice_fusion.11
  460.2 3.1 rev.85
  464.8 22.5 %add_add_fusion.7 = f32[128,512]{0,1:T(8,128)S(1)} fusion(f32[128,512]{0,1:T(8,128)} %rev.85, f32[]{:T(128)} %bitcast.462, f32[]{:T(128)} %bitcast.463, f32[]{:T(128)} %bitcast.464, f32[]{:T(128)} %bitcast.465, f32[]{:T(128)} %bitcast.466, f32[]{:T(128)} %bitcast.467, f32[]{:T(128)} %bitcast.468, f32[]{:T(128)} %bitcast.469, f32[]{:T(128)} %bitcast.470, ...), kind=kLoop, calls=%fused_computation.100.clone.1 | loop fusion | flops 12451840 | bytes 526976 | tf_op jit(solution)/shard_map/while/body/eval_jaxpr/while/body/eval_jaxpr/jvp()/add | solution.py:45
  499.2 2.5 select_reduce_fusion.33
  501.8 20.1 %fusion.230 = f32[32]{0:T(128)S(1)} fusion(f32[32]{0:T(128)S(1)} %get-tuple-element.2032, pred[]{:T(512)S(6)} %compare.44, f32[1]{0:T(128)} %bitcast.498, f32[1]{0:T(128)} %bitcast.499, f32[1]{0:T(128)} %bitcast.500, f32[1]{0:T(128)} %bitcast.501, f32[1]{0:T(128)} %bitcast.502, f32[1]{0:T(128)} %bitcast.503, f32[1]{0:T(128)} %bitcast.504, ...), kind=kLoop, calls=%fused_computation.175.clone.1 | loop fusion | flops 1056 | bytes 385 | tf_op jit(solution)/shard_map/while/body/eval_jaxpr/while/body/eval_jaxpr/add | solution.py:202
  523.1 141.6 %all-reduce.34 = (f32[1024]{0:T(1024)}, f32[32]{0:T(128)}) all-reduce(f32[1024]{0:T(1024)S(1)} %get-tuple-element.956, f32[32]{0:T(128)S(1)} %get-tuple-element.957), channel_id=1, replica_groups=mesh['dp'=64,'ctx'=8] {'dp','ctx'}, use_global_device_ids=true, to_apply=%region_48.49 | all-reduce | flops 1056 | bytes 8448 | tf_op jit(solution)/shard_map/psum | solution.py:278
  664.7 3.0 fusion.136
  668.5 88.4 %while.80 = (s32[]{:T(128)}, f32[128,1024]{0,1:T(8,128)}, f32[128,1024]{0,1:T(8,128)}, s32[2]{0:T(128)S(1)}, bf16[1024,1024]{0,1:T(8,128)(2,1)}, /*index=5*/s32[...) while((s32[]{:T(128)}, f32[128,1024]{0,1:T(8,128)}, ...), condition=%wide.region_45.46_spmd.clone, body=%wide.region_44.45_spmd.clone.sunk | while | flops 560531328 | bytes 61329784 | solution.py:266
  679.0 21.7 %add_add_fusion.8 = f32[512,128]{1,0:T(8,128)S(1)} fusion(f32[512,128]{1,0:T(8,128)S(1)} %rev.87, f32[]{:T(128)} %bitcast.541, f32[]{:T(128)} %bitcast.542, f32[]{:T(128)} %bitcast.543, f32[]{:T(128)} %bitcast.544, f32[]{:T(128)} %bitcast.545, f32[]{:T(128)} %bitcast.546, f32[]{:T(128)} %bitcast.547, f32[]{:T(128)} %bitcast.548, f32[]{:T(128)} %bitcast.549, ...), kind=kLoop, calls=%fused_computation.195.clone.1 | loop fusion | flops 12451840 | bytes 526976 | tf_op jit(solution)/shard_map/while/body/eval_jaxpr/while/body/eval_jaxpr/jvp()/add | solution.py:45
  701.0 3.8 fusion.241
  706.6 3.6 fusion.242
  723.0 21.7 %add_add_fusion.8 = f32[512,128]{1,0:T(8,128)S(1)} fusion(f32[512,128]{1,0:T(8,128)S(1)} %rev.87, f32[]{:T(128)} %bitcast.541, f32[]{:T(128)} %bitcast.542, f32[]{:T(128)} %bitcast.543, f32[]{:T(128)} %bitcast.544, f32[]{:T(128)} %bitcast.545, f32[]{:T(128)} %bitcast.546, f32[]{:T(128)} %bitcast.547, f32[]{:T(128)} %bitcast.548, f32[]{:T(128)} %bitcast.549, ...), kind=kLoop, calls=%fused_computation.195.clone.1 | loop fusion | flops 12451840 | bytes 526976 | tf_op jit(solution)/shard_map/while/body/eval_jaxpr/while/body/eval_jaxpr/jvp()/add | solution.py:45
  745.1 3.8 fusion.241
  750.6 3.6 fusion.242
  754.2 2.6 bitcast_add_fusion.11
  760.7 5.2 reduce-scatter.2.cloned.1.call-done
  766.0 65.4 %all-gather.3 = f32[128,1024]{1,0:T(8,128)S(1)} all-gather(f32[16,1024]{1,0:T(8,128)} %reduce-scatter.2.cloned.1.call-done), channel_id=5, replica_groups=mesh['dp'=64,'ctx'=8] {'ctx'}, dimensions={0}, use_global_device_ids=true | all-gather | bytes 589824 | tf_op jit(solution)/shard_map/all_gather | solution.py:12
  (271 shorter events, 111.1 us)
Async XLA Ops:
  7.2 355.9 %copy-start = (bf16[1,128,1024]{2,1,0:T(8,128)(2,1)S(1)}, bf16[1,128,1024]{2,1,0:T(8,128)(2,1)}, u32[]{:S(2)}) copy-start(bf16[1,128,1024]{2,1,0:T(8,128)(2,1)} %param.20) | copy-start | bytes 786436
  7.2 6.5 copy-start.18
  7.2 6.8 copy-start.17
  7.2 96.8 %copy-start.16 = (f32[1024]{0:T(1024)S(1)}, f32[1024]{0:T(1024)}, u32[]{:S(2)}) copy-start(f32[1024]{0:T(1024)} %param.24) | copy-start | bytes 12292
  7.2 96.8 %copy-start.1 = (f32[32]{0:T(128)S(1)}, f32[32]{0:T(128)}, u32[]{:S(2)}) copy-start(f32[32]{0:T(128)} %param.25) | copy-start | bytes 388
  7.2 52.6 %all-gather.14.cloned.1.call-start = ((), (), s32[]{:S(2)}) async-start(), calls=%async_computation.4 | async-start | bytes 2359296 | tf_op jit(solution)/shard_map/all_gather | solution.py:115
  9.1 94.9 %all-gather.16.cloned.1.call-start = ((), (), s32[]{:S(2)}) async-start(), calls=%async_computation.5 | async-start | bytes 2359296 | tf_op jit(solution)/shard_map/all_gather | solution.py:114
  11.0 352.0 %all-gather.10.cloned.1.call-start = ((), (), s32[]{:S(2)}) async-start(), calls=%async_computation.1 | async-start | bytes 2129920 | tf_op jit(solution)/shard_map/all_gather | solution.py:153
  11.7 656.7 %all-gather.18.cloned.1.call-start = ((), (), s32[]{:S(2)}) async-start(), calls=%async_computation.6 | async-start | bytes 2359296 | tf_op jit(solution)/shard_map/all_gather | solution.py:227
  13.6 654.9 %all-gather.12.cloned.1.call-start = ((), (), s32[]{:S(2)}) async-start(), calls=%async_computation.2 | async-start | bytes 2359296 | tf_op jit(solution)/shard_map/all_gather | solution.py:228
  133.3 3.0 copy-start.8
  167.6 3.0 copy-start.8
  173.8 193.1 %copy-start.11 = (bf16[128,1024]{1,0:T(8,128)(2,1)}, bf16[128,1024]{1,0:T(8,128)(2,1)S(1)}, u32[]{:S(2)}) copy-start(bf16[128,1024]{1,0:T(8,128)(2,1)S(1)} %copy.114) | copy-start | bytes 786436
  173.9 191.7 %copy-start.14 = (bf16[1,128,1024]{2,1,0:T(8,128)(2,1)S(1)}, bf16[1,128,1024]{2,1,0:T(8,128)(2,1)}, u32[]{:S(2)}) copy-start(bf16[1,128,1024]{2,1,0:T(8,128)(2,1)} %param.19) | copy-start | bytes 786436
  366.7 399.3 %reduce-scatter.2.cloned.1.call-start = ((), (), s32[]{:S(2)}) async-start(), calls=%async_computation.3 | async-start | bytes 4259840 | tf_op jit(solution)/shard_map/reduce_scatter | solution.py:158
  369.7 1.6 copy-start.4
  412.1 2.0 copy-start.6
  412.1 2.0 copy-start.15
  419.3 4.6 copy-start.7
  487.3 1.9 copy-start.6
  487.3 2.0 copy-start.15
  494.6 4.6 copy-start.7
  669.7 2.8 copy-start.10
  672.6 3.0 copy-start.2
  700.7 4.1 copy-start.13
  701.0 5.5 copy-start.3
  701.0 5.5 copy-start.5
  713.7 2.8 copy-start.10
  716.7 3.0 copy-start.2
  744.7 4.1 copy-start.13
  745.1 5.5 copy-start.3
  745.1 5.5 copy-start.5
  (4 other events, 3.5 us)
Sparse Core Ops, SparseCore 0:
  10.7 49.0 all-gather.13
  62.5 41.4 all-gather.15
  106.1 256.8 all-gather.9
  365.0 83.7 all-gather.17
  451.4 37.0 all-gather.11
  491.1 274.8 reduce-scatter.1
